TPU v7x, 256 devices: a whole 4x4x8 slice. The times are simulated.
256 devices in a mesh: row: 8 (over z_lo, y), col: 32 (over z_hi, x, core).
Axes of the slice: x: 4, y: 4, z: 8 (z_hi: 4, z_lo: 2; z = z_hi * 2 + z_lo), core: 2. Of those that a mesh axis runs over, the one named last changes fastest.
Arguments:
- tokens: bfloat16 [512, 12288], P('col', 'row'), may hold values from -6 to 6
- grad_out: bfloat16 [512, 12288], P('col', 'row'), may hold values from -6 to 6
- weight_in: bfloat16 [12288, 24576], P('row', 'col'), may hold values from -0.0546875 to 0.0546875
- weight_out: bfloat16 [24576, 12288], P('col', 'row'), may hold values from -0.0390625 to 0.0390625
Outputs:
- output: bfloat16 [512, 12288], P('col', 'row')
- grad_in: bfloat16 [512, 12288], P('col', 'row')
- grad_w_in: bfloat16 [12288, 24576], P('row', 'col')
- grad_w_out: bfloat16 [24576, 12288], P('col', 'row')
All inputs are finite; a program needn't handle non-finite values.
Results may differ from a plain program's by a relative error of at most 0.02.
Values may be sent and summed in bfloat16 or wider, within the bound.
A program may use at most 64 MiB of HBM per device.

v0:
```python
import math

import jax
import jax.numpy as jnp
from jax import lax
from jax.sharding import PartitionSpec as P

root_two_pi = math.sqrt(2.0 / math.pi)


def gelu_value(pre):
    inner = root_two_pi * (pre + 0.044715 * pre * pre * pre)
    return 0.5 * pre * (1.0 + jnp.tanh(inner))


def gelu_slope(pre):
    inner = root_two_pi * (pre + 0.044715 * pre * pre * pre)
    bent = jnp.tanh(inner)
    return 0.5 * (1.0 + bent) + 0.5 * pre * (1.0 - bent * bent) * root_two_pi * (
        1.0 + 3.0 * 0.044715 * pre * pre
    )


def times_transposed(left, right):
    return lax.dot_general(
        left, right, (((1,), (1,)), ((), ())), preferred_element_type=jnp.float32
    )


def inner_tokens(left, right):
    return lax.dot_general(
        left, right, (((0,), (0,)), ((), ())), preferred_element_type=jnp.float32
    )


def shards(tokens, grad_out, weight_in, weight_out):
    token_panel, grad_panel = (
        lax.all_gather(tokens, "col", axis=0, tiled=True),
        lax.all_gather(grad_out, "col", axis=0, tiled=True),
    )
    total_rows = token_panel.shape[0]
    width_hidden = weight_in.shape[1]
    grad_rows = grad_panel
    forward = jnp.dot(token_panel, weight_in, preferred_element_type=jnp.float32)
    backward = times_transposed(grad_rows, weight_out)
    summed = lax.psum_scatter(
        jnp.concatenate([forward, backward], axis=1), "row", scatter_dimension=0, tiled=True
    )
    hidden_pre = summed[:, :width_hidden]
    hidden_act = gelu_value(hidden_pre).astype(jnp.bfloat16)
    pre_grad = (summed[:, width_hidden:] * gelu_slope(hidden_pre)).astype(jnp.bfloat16)
    act_panel, pregrad_panel = (
        lax.all_gather(hidden_act, "row", axis=0, tiled=True),
        lax.all_gather(pre_grad, "row", axis=0, tiled=True),
    )
    factor = 1.0 / math.sqrt(total_rows)
    output = lax.psum_scatter(
        jnp.dot(act_panel, weight_out, preferred_element_type=jnp.float32).astype(jnp.bfloat16),
        "col",
        scatter_dimension=0,
        tiled=True,
    )
    grad_w_out = (inner_tokens(act_panel, grad_panel) * factor).astype(jnp.bfloat16)
    grad_rows = pregrad_panel
    grad_in = lax.psum_scatter(
        times_transposed(grad_rows, weight_in).astype(jnp.bfloat16),
        "col",
        scatter_dimension=0,
        tiled=True,
    )
    grad_w_in = (inner_tokens(token_panel, pregrad_panel) * factor).astype(jnp.bfloat16)
    return (output, grad_in, grad_w_in, grad_w_out)


def solution(mesh):
    placed = (P("col", "row"), P("col", "row"), P("row", "col"), P("col", "row"))
    return jax.shard_map(
        shards,
        mesh=mesh,
        in_specs=placed,
        out_specs=(P("col", "row"), P("col", "row"), P("row", "col"), P("col", "row")),
        check_vma=False,
    )
```

profile of v0, /device:TPU:1, one launch (start us, length us, event | category | flops | bytes accessed | tf_op | source)
XLA Modules:
  0.0 392.0 jit_solution(12617767968671838270)
XLA Ops:
  7.2 0.0 copy-start
  7.2 0.0 all-gather.5.cloned.1.call-start
  7.2 0.7 all-gather.5.cloned.1.call-update
  7.9 0.0 all-gather.3.cloned.1.call-start
  8.0 0.7 all-gather.3.cloned.1.call-update
  8.7 0.0 reduce-scatter.4.cloned.1.call-start
  8.7 59.2 %all-gather.5.cloned.1.call-done = bf16[512,1536]{1,0:T(8,128)(2,1)} async-done(((bf16[16,1536]{1,0:T(8,128)(2,1)}), bf16[512,1536]{1,0:T(8,128)(2,1)}) %all-gather.5.cloned.1.call-update) | async-done | bytes 1572880 | tf_op jit(solution)/shard_map/all_gather | solution.py:39
  67.9 0.0 copy-done
  67.9 4.0 %fusion.9 = f32[512,768]{1,0:T(8,128)} fusion(bf16[512,1536]{1,0:T(8,128)(2,1)} %all-gather.5.cloned.1.call-done, bf16[768,1536]{1,0:T(8,128)(2,1)S(1)} %copy-done), kind=kOutput, calls=%fused_computation.17 | convolution fusion | flops 1207959552 | bytes 5505024 | tf_op jit(solution)/shard_map/dot_general | solution.py:25
  71.9 48.9 %all-gather.3.cloned.1.call-done = bf16[512,1536]{1,0:T(8,128)(2,1)} async-done(((bf16[16,1536]{1,0:T(8,128)(2,1)}), bf16[512,1536]{1,0:T(8,128)(2,1)}) %all-gather.3.cloned.1.call-update) | async-done | bytes 1572880 | tf_op jit(solution)/shard_map/all_gather | solution.py:38
  120.8 0.0 copy-start.1
  120.8 3.6 fusion.8
  124.5 0.0 copy-done.1
  124.5 2.0 pad_maximum_fusion
  126.5 0.0 reduce-scatter.4.cloned.1.call-update
  126.5 0.0 reduce-scatter.6.cloned.1.call-start
  126.6 41.7 %reduce-scatter.4.cloned.1.call-done = f32[64,1536]{1,0:T(8,128)} async-done(((f32[512,1536]{1,0:T(8,128)}), f32[64,1536]{1,0:T(8,128)}) %reduce-scatter.4.cloned.1.call-update) | async-done | bytes 393232 | tf_op jit(solution)/shard_map/reduce_scatter | solution.py:46
  168.3 1.2 fusion.7
  169.4 24.4 %all_gather.14 = bf16[512,768]{1,0:T(8,128)(2,1)S(1)} all-gather(bf16[64,768]{1,0:T(8,128)(2,1)S(1)} %get-tuple-element.9), channel_id=1, replica_groups=mesh['row'=8,'col'=32] {'row'}, dimensions={0}, use_global_device_ids=true | all-gather | bytes 884736 | tf_op jit(solution)/shard_map/all_gather | solution.py:53
  193.9 2.5 convolution_convert_fusion.1
  196.4 0.0 reduce-scatter.6.cloned.1.call-update
  196.4 0.0 reduce-scatter.8.cloned.1.call-start
  196.5 23.7 %all_gather.15 = bf16[512,768]{1,0:T(8,128)(2,1)S(1)} all-gather(bf16[64,768]{1,0:T(8,128)(2,1)S(1)} %get-tuple-element.8), channel_id=1, replica_groups=mesh['row'=8,'col'=32] {'row'}, dimensions={0}, use_global_device_ids=true | all-gather | bytes 884736 | tf_op jit(solution)/shard_map/all_gather | solution.py:54
  220.2 0.0 copy-start.2
  220.2 0.9 copy-done.2
  221.1 4.3 %convolution_convert_fusion = bf16[512,1536]{1,0:T(8,128)(2,1)} fusion(bf16[512,768]{1,0:T(8,128)(2,1)S(1)} %all_gather.15, bf16[1536,768]{1,0:T(8,128)(2,1)} %param.6), kind=kOutput, calls=%fused_computation.4 | convolution fusion | flops 1208745984 | bytes 4718592 | tf_op jit(solution)/shard_map/dot_general | solution.py:25
  225.4 0.0 reduce-scatter.8.cloned.1.call-update
  225.4 4.5 %fusion = bf16[1536,768]{0,1:T(8,128)(2,1)} fusion(bf16[512,768]{1,0:T(8,128)(2,1)} %copy-done.2, bf16[512,1536]{1,0:T(8,128)(2,1)} %all-gather.3.cloned.1.call-done), kind=kOutput, calls=%fused_computation.3 | convolution fusion | flops 1210318848 | bytes 4718592 | tf_op jit(solution)/shard_map/dot_general | solution.py:31
  229.9 4.3 %copy.8 = bf16[1536,768]{1,0:T(8,128)(2,1)} copy(bf16[1536,768]{0,1:T(8,128)(2,1)} %fusion) | data formatting | bytes 4718592
  234.2 4.2 %multiply_convert_fusion = bf16[768,1536]{1,0:T(8,128)(2,1)} fusion(bf16[512,768]{1,0:T(8,128)(2,1)S(1)} %all_gather.14, bf16[512,1536]{1,0:T(8,128)(2,1)} %all-gather.5.cloned.1.call-done), kind=kOutput, calls=%fused_computation | convolution fusion | flops 1210318848 | bytes 4718592 | tf_op jit(solution)/shard_map/dot_general | solution.py:31
  238.4 54.9 %reduce-scatter.6.cloned.1.call-done = bf16[16,1536]{1,0:T(8,128)(2,1)} async-done(((bf16[512,1536]{1,0:T(8,128)(2,1)}), bf16[16,1536]{1,0:T(8,128)(2,1)}) %reduce-scatter.6.cloned.1.call-update) | async-done | bytes 49168 | tf_op jit(solution)/shard_map/reduce_scatter | solution.py:57
  293.4 92.1 %reduce-scatter.8.cloned.1.call-done = bf16[16,1536]{1,0:T(8,128)(2,1)} async-done(((bf16[512,1536]{1,0:T(8,128)(2,1)}), bf16[16,1536]{1,0:T(8,128)(2,1)}) %reduce-scatter.8.cloned.1.call-update) | async-done | bytes 49168 | tf_op jit(solution)/shard_map/reduce_scatter | solution.py:65
Async XLA Ops:
  7.2 60.8 %copy-start = (bf16[768,1536]{1,0:T(8,128)(2,1)S(1)}, bf16[768,1536]{1,0:T(8,128)(2,1)}, u32[]{:S(2)}) copy-start(bf16[768,1536]{1,0:T(8,128)(2,1)} %param.7) | copy-start | bytes 7077892
  7.2 60.8 %all-gather.5.cloned.1.call-start = ((), (), s32[]{:S(2)}) async-start(), calls=%async_computation.4 | async-start | bytes 1622016 | tf_op jit(solution)/shard_map/all_gather | solution.py:39
  7.9 112.9 %all-gather.3.cloned.1.call-start = ((), (), s32[]{:S(2)}) async-start(), calls=%async_computation.3 | async-start | bytes 1622016 | tf_op jit(solution)/shard_map/all_gather | solution.py:38
  8.7 159.6 %reduce-scatter.4.cloned.1.call-start = ((), (), s32[]{:S(2)}) async-start(), calls=%async_computation.5 | async-start | bytes 3538944 | tf_op jit(solution)/shard_map/reduce_scatter | solution.py:46
  120.8 3.6 copy-start.1
  126.5 166.9 %reduce-scatter.6.cloned.1.call-start = ((), (), s32[]{:S(2)}) async-start(), calls=%async_computation.6 | async-start | bytes 1622016 | tf_op jit(solution)/shard_map/reduce_scatter | solution.py:57
  196.4 189.0 %reduce-scatter.8.cloned.1.call-start = ((), (), s32[]{:S(2)}) async-start(), calls=%async_computation.7 | async-start | bytes 1622016 | tf_op jit(solution)/shard_map/reduce_scatter | solution.py:65
  220.2 0.9 copy-start.2
Sparse Core Ops, SparseCore 0:
  10.6 57.3 all-gather.4
  70.5 50.2 all-gather.2
  126.6 41.6 reduce-scatter.3
  196.6 96.7 reduce-scatter.5
  297.6 87.7 reduce-scatter.7
where the time goes:
time: 393 us; the launch traced here: 392 us
  waiting for transfers between devices  298 us (76%)
  blocking collectives  48.1 us (12%)
  matrix products  23.2 us (6%)
  between operations  13.8 us (4%)
  local copies, waits for them, and re-layouts  5.19 us (1%)
    reduce_scatter x1, waiting for transfers between devices, shards(): lax.psum_scatter(times_transposed(grad_rows, weight_in).astype(jnp.bfloat...  92.1 us
    all_gather x1, waiting for transfers between devices, shards(): lax.all_gather(grad_out, 'col', axis=0, tiled=True)  59.2 us
    reduce_scatter x1, waiting for transfers between devices, shards(): lax.psum_scatter(jnp.dot(act_panel, weight_out, preferred_element_type=jn...  54.9 us
    all_gather x1, waiting for transfers between devices, shards(): lax.all_gather(tokens, 'col', axis=0, tiled=True)  48.9 us
    reduce_scatter x1, waiting for transfers between devices, shards(): lax.psum_scatter(jnp.concatenate([forward, backward], axis=1), 'row', sca...  41.7 us
    all_gather x1, blocking collectives, shards(): lax.all_gather(hidden_act, 'row', axis=0, tiled=True)  24.4 us
    all_gather x1, blocking collectives, shards(): lax.all_gather(pre_grad, 'row', axis=0, tiled=True)  23.7 us
    dot_general x2, matrix products, inner_tokens(): lax.dot_general(left, right, (((0,), (0,)), ((), ())), preferred_element_...  8.76 us
  transfers between devices with their start and end apart: 5, of which 5 were waited for; matrix products, arithmetic and copies ran while one was open for 5% of the time, Pallas kernels for 0%

commit v1 on v0

v1 whole, which is shorter than its diff:
```python
import math

import jax
import jax.numpy as jnp
from jax import lax
from jax.experimental import pallas as pl
from jax.experimental.pallas import tpu as pltpu
from jax.sharding import PartitionSpec as P

root_two_pi = math.sqrt(2.0 / math.pi)
BF = jnp.bfloat16
F32 = jnp.float32
NT = (((1,), (1,)), ((), ()))
TN = (((0,), (0,)), ((), ()))
CHUNKS = (0, 1, 3, 2)
AWAY = (1, 3, 2)
TILE = 256


def gelu_pair(pre, grad):
    inner = root_two_pi * (pre + 0.044715 * pre * pre * pre)
    bent = jnp.tanh(inner)
    act = 0.5 * pre * (1.0 + bent)
    slope = 0.5 * (1.0 + bent) + 0.5 * pre * (1.0 - bent * bent) * root_two_pi * (
        1.0 + 3.0 * 0.044715 * pre * pre
    )
    return act, grad * slope


def kernel(
    tokens, grad_out, weight_in, weight_out,
    output, grad_in, grad_w_in, grad_w_out,
    panel, w_in, w_out, part, y_recv, z_send, z_own, z_recv, hidden,
    o_part, o_recv, x_send, x_recv, e_send, e_recv, final, gw_in, gw_out,
    load_sem, store_sem, gi_sem, go_sem,
    ag_recv, agz_send, agx_send, sib_recv, sib_send,
    y_rs, y_ss, z_rs, z_ss, p_rs, p_ss, hy_rs, hy_ss,
    o_rs, o_ss, x_rs, x_ss, e_rs, e_ss,
):
    row, col = lax.axis_index("row"), lax.axis_index("col")
    y, low = lax.rem(row, 4), lax.div(row, 4)
    core, x, z = lax.rem(col, 2), lax.rem(lax.div(col, 2), 4), lax.div(col, 8)

    def around(place, step):
        return lax.rem(place + step, 4)

    sibling = (row, z * 8 + x * 2 + (1 - core))
    partner = ((1 - low) * 4 + y, col)
    x_peer = {d: (row, z * 8 + around(x, d) * 2 + core) for d in AWAY}
    z_peer = {d: (row, around(z, d) * 8 + x * 2 + core) for d in AWAY}
    y_peer = {d: (low * 4 + around(y, d), col) for d in AWAY}
    sends = []

    def send(src, dst, send_sem, recv_sem, device):
        copy = pltpu.make_async_remote_copy(
            src_ref=src, dst_ref=dst, send_sem=send_sem, recv_sem=recv_sem,
            device_id=device, device_id_type=pl.DeviceIdType.MESH,
        )
        copy.start()
        sends.append(copy)

    def arrived(dst, send_sem, recv_sem, device):
        pltpu.make_async_remote_copy(
            src_ref=dst, dst_ref=dst, send_sem=send_sem, recv_sem=recv_sem,
            device_id=device, device_id_type=pl.DeviceIdType.MESH,
        ).wait_recv()

    own = panel.at[x, z, core]
    loads = [
        pltpu.make_async_copy(tokens, panel.at[x, z, core, 0], load_sem.at[0]),
        pltpu.make_async_copy(grad_out, panel.at[x, z, core, 1], load_sem.at[1]),
        pltpu.make_async_copy(weight_in, w_in, load_sem.at[2]),
        pltpu.make_async_copy(weight_out, w_out, load_sem.at[3]),
    ]
    for load in loads:
        load.start()
    peers = [sibling, partner] + [p[d] for p in (x_peer, z_peer, y_peer) for d in AWAY]
    barrier = pltpu.get_barrier_semaphore()
    for peer in peers:
        pl.semaphore_signal(barrier, inc=1, device_id=peer, device_id_type=pl.DeviceIdType.MESH)
    pl.semaphore_wait(barrier, len(peers))
    loads[0].wait()
    loads[1].wait()

    def to_sibling(dx, dz):
        block = panel.at[around(x, dx), around(z, dz), core]
        send(block, block, sib_send.at[dx, dz], sib_recv.at[dx, dz], sibling)

    def along_x(dz):
        block = panel.at[x, around(z, dz), core]
        for d in AWAY:
            send(block, block, agx_send.at[d, dz], ag_recv.at[4 - d, dz], x_peer[d])

    def gather_start():
        for d in AWAY:
            send(own, own, agz_send.at[d], ag_recv.at[0, 4 - d], z_peer[d])
        to_sibling(0, 0)
        along_x(0)

    def gather(dx, dz):
        block = panel.at[around(x, dx), around(z, dz), core]
        arrived(block, sib_send.at[dx, dz], ag_recv.at[dx, dz], sibling)
        to_sibling(dx, dz)
        if dx == 0:
            along_x(dz)

    def first(i):
        dx = CHUNKS[i]
        xk = around(x, dx)
        for dz in range(4):
            block = panel.at[xk, around(z, dz), 1 - core]
            arrived(block, sib_send.at[dx, dz], sib_recv.at[dx, dz], sibling)

        @pl.loop(0, 768 // TILE)
        def _(n):
            cols = pl.ds(pl.multiple_of(n * TILE, TILE), TILE)
            left = panel[xk, :, :, 0].reshape(128, 1536)
            pre = jnp.dot(left, w_in[:, cols], preferred_element_type=F32)
            part[i, :, :, 0, :, cols] = pre.astype(BF).reshape(4, 2, 16, TILE)
            left = panel[xk, :, :, 1].reshape(128, 1536)
            grad = lax.dot_general(left, w_out[cols, :], NT, preferred_element_type=F32)
            part[i, :, :, 1, :, cols] = grad.astype(BF).reshape(4, 2, 16, TILE)

        for d in AWAY:
            send(
                part.at[i, around(y, d)], y_recv.at[i, 3 - d],
                y_ss.at[i, d - 1], y_rs.at[i, 3 - d], y_peer[d],
            )

    def sum_y(i):
        for d in AWAY:
            arrived(y_recv.at[i, d - 1], y_ss.at[i, d - 1], y_rs.at[i, d - 1], sibling)

        def total(which):
            t = part[i, y, which].astype(F32)
            for j in range(3):
                t = t + y_recv[i, j, which].astype(F32)
            return t

        z_send[i] = total(1 - low).astype(BF)
        send(z_send.at[i], z_recv.at[i], z_ss.at[i], z_rs.at[i], partner)
        z_own[i] = total(low)

    def bend(i):
        xk = around(x, CHUNKS[i])
        arrived(z_recv.at[i], z_ss.at[i], z_rs.at[i], partner)
        total = z_own[i] + z_recv[i].astype(F32)
        act, pre_grad = gelu_pair(total[0], total[1])
        hidden[xk, y, low, 0] = act.astype(BF)
        hidden[xk, y, low, 1] = pre_grad.astype(BF)
        block = hidden.at[xk, y, low]
        send(block, block, p_ss.at[i], p_rs.at[i], partner)
        for d in AWAY:
            send(block, block, hy_ss.at[i, 0, d - 1], hy_rs.at[i, 0, 3 - d], y_peer[d])

    def pass_on(i):
        block = hidden.at[around(x, CHUNKS[i]), y, 1 - low]
        arrived(block, p_ss.at[i], p_rs.at[i], partner)
        for d in AWAY:
            send(block, block, hy_ss.at[i, 1, d - 1], hy_rs.at[i, 1, 3 - d], y_peer[d])

    def second(i):
        xk = around(x, CHUNKS[i])
        for d in AWAY:
            for k, half in ((0, low), (1, 1 - low)):
                block = hidden.at[xk, around(y, d), half]
                arrived(block, hy_ss.at[i, k, d - 1], hy_rs.at[i, k, d - 1], partner)

        @pl.loop(0, 1536 // TILE)
        def _(n):
            cols = pl.ds(pl.multiple_of(n * TILE, TILE), TILE)
            left = hidden[xk, :, :, 0].reshape(128, 768)
            out = jnp.dot(left, w_out[:, cols], preferred_element_type=F32)
            out = out.astype(BF).reshape(4, 2, 16, TILE)
            left = hidden[xk, :, :, 1].reshape(128, 768)
            back = lax.dot_general(left, w_in[cols, :], NT, preferred_element_type=F32)
            back = back.astype(BF).reshape(4, 2, 16, TILE)
            for c in range(2):
                o_part[i, c, :, 0, :, cols] = out[:, c]
                o_part[i, c, :, 1, :, cols] = back[:, c]

        send(o_part.at[i, 1 - core], o_recv.at[i], o_ss.at[i], o_rs.at[i], sibling)

    def sum_core(i):
        arrived(o_recv.at[i], o_ss.at[i], o_rs.at[i], sibling)

        @pl.loop(0, 4)
        def _(k):
            total = o_part[i, core, k].astype(F32) + o_recv[i, k].astype(F32)
            x_send[i, k] = total.astype(BF)

        if i > 0:
            d = CHUNKS[i]
            send(x_send.at[i], x_recv.at[3 - d], x_ss.at[d - 1], x_rs.at[3 - d], x_peer[d])

    def sum_x():
        for d in AWAY:
            arrived(x_recv.at[d - 1], x_ss.at[d - 1], x_rs.at[d - 1], sibling)
        for dz in AWAY + (0,):
            zk = around(z, dz)
            total = x_send[0, zk].astype(F32)
            for j in range(3):
                total = total + x_recv[j, zk].astype(F32)
            e_send[dz] = total.astype(BF)
            if dz > 0:
                send(
                    e_send.at[dz], e_recv.at[3 - dz], e_ss.at[dz - 1], e_rs.at[3 - dz], z_peer[dz]
                )

    def sum_z():
        for d in AWAY:
            arrived(e_recv.at[d - 1], e_ss.at[d - 1], e_rs.at[d - 1], sibling)
        total = e_send[0].astype(F32)
        for j in range(3):
            total = total + e_recv[j].astype(F32)
        final[...] = total.astype(BF)

    factor = 1.0 / math.sqrt(512)

    def gw_in_store(m):
        rows = pl.ds(pl.multiple_of(m * TILE, TILE), TILE)
        return pltpu.make_async_copy(gw_in.at[rows], grad_w_in.at[rows], gi_sem.at[m])

    def gw_out_store(m):
        rows = pl.ds(pl.multiple_of(m * TILE, TILE), TILE)
        return pltpu.make_async_copy(gw_out.at[rows], grad_w_out.at[rows], go_sem.at[m])

    def weight_in_grad(low_m, high_m):
        @pl.loop(low_m, high_m)
        def _(m):
            cols = pl.ds(pl.multiple_of(m * TILE, TILE), TILE)
            left = panel[:, :, :, 0, :, cols].reshape(512, TILE)
            right = hidden[:, :, :, 1].reshape(512, 768)
            grad = lax.dot_general(left, right, TN, preferred_element_type=F32)
            gw_in[cols, :] = (grad * factor).astype(BF)
            gw_in_store(m).start()

    def weight_out_grad(low_m, high_m):
        @pl.loop(low_m, high_m)
        def _(m):
            cols = pl.ds(pl.multiple_of(m * TILE, TILE), TILE)
            left = hidden[:, :, :, 0, :, cols].reshape(512, TILE)
            right = panel[:, :, :, 1].reshape(512, 1536)
            grad = lax.dot_general(left, right, TN, preferred_element_type=F32)
            gw_out[cols, :] = (grad * factor).astype(BF)
            gw_out_store(m).start()

    gather_start()
    for dz in AWAY:
        gather(0, dz)
    loads[2].wait()
    loads[3].wait()
    first(0)
    for dz in (0,) + AWAY:
        gather(1, dz)
        gather(3, dz)
    first(1)
    sum_y(0)
    first(2)
    for dz in (0,) + AWAY:
        gather(2, dz)
    bend(0)
    sum_y(1)
    first(3)
    pass_on(0)
    bend(1)
    sum_y(2)
    second(0)
    pass_on(1)
    bend(2)
    sum_y(3)
    sum_core(0)
    second(1)
    pass_on(2)
    bend(3)
    sum_core(1)
    second(2)
    pass_on(3)
    sum_core(2)
    second(3)
    weight_in_grad(0, 2)
    sum_core(3)
    weight_in_grad(2, 6)
    weight_out_grad(0, 2)
    sum_x()
    weight_out_grad(2, 3)
    sum_z()
    stores = [
        pltpu.make_async_copy(final.at[0], output, store_sem.at[0]),
        pltpu.make_async_copy(final.at[1], grad_in, store_sem.at[1]),
    ]
    for store in stores:
        store.start()
    for m in range(6):
        gw_in_store(m).wait()
    for m in range(3):
        gw_out_store(m).wait()
    for store in stores:
        store.wait()
    for copy in sends:
        copy.wait_send()


def shards(tokens, grad_out, weight_in, weight_out):
    dma = pltpu.SemaphoreType.DMA
    vmem = pltpu.VMEM
    like = jax.ShapeDtypeStruct
    return pl.pallas_call(
        kernel,
        out_shape=(
            like(tokens.shape, BF),
            like(tokens.shape, BF),
            like(weight_in.shape, BF),
            like(weight_out.shape, BF),
        ),
        in_specs=[pl.BlockSpec(memory_space=pl.ANY)] * 4,
        out_specs=[pl.BlockSpec(memory_space=pl.ANY)] * 4,
        scratch_shapes=[
            vmem((4, 4, 2, 2, 16, 1536), BF),
            vmem((1536, 768), BF),
            vmem((768, 1536), BF),
            vmem((4, 4, 2, 2, 16, 768), BF),
            vmem((4, 3, 2, 2, 16, 768), BF),
            vmem((4, 2, 16, 768), BF),
            vmem((4, 2, 16, 768), F32),
            vmem((4, 2, 16, 768), BF),
            vmem((4, 4, 2, 2, 16, 768), BF),
            vmem((4, 2, 4, 2, 16, 1536), BF),
            vmem((4, 4, 2, 16, 1536), BF),
            vmem((4, 4, 2, 16, 1536), BF),
            vmem((3, 4, 2, 16, 1536), BF),
            vmem((4, 2, 16, 1536), BF),
            vmem((3, 2, 16, 1536), BF),
            vmem((2, 16, 1536), BF),
            vmem((1536, 768), BF),
            vmem((768, 1536), BF),
            dma((4,)), dma((2,)), dma((6,)), dma((3,)),
            dma((4, 4)), dma((4,)), dma((4, 4)), dma((4, 4)), dma((4, 4)),
            dma((4, 3)), dma((4, 3)), dma((4,)), dma((4,)), dma((4,)), dma((4,)),
            dma((4, 2, 3)), dma((4, 2, 3)),
            dma((4,)), dma((4,)), dma((3,)), dma((3,)), dma((3,)), dma((3,)),
        ],
        compiler_params=pltpu.CompilerParams(
            collective_id=0, has_side_effects=True, vmem_limit_bytes=48 * 2**20
        ),
        name="block",
    )(tokens, grad_out, weight_in, weight_out)


def solution(mesh):
    placed = (P("col", "row"), P("col", "row"), P("row", "col"), P("col", "row"))
    return jax.shard_map(
        shards, mesh=mesh, in_specs=placed, out_specs=placed, check_vma=False
    )
```

time: 393 us -> 107 us (0.27)
  waiting for transfers between devices: 298 us -> 0 us
  Pallas kernels: 0 us -> 99.5 us
  blocking collectives: 48.1 us -> 0 us
  matrix products: 23.2 us -> 0 us
  between operations: 13.8 us -> 0.65 us
    reduce_scatter x3 -> x0, waiting for transfers between devices: 189 us -> none  [the longest x1 92.1 us: shards(): lax.psum_scatter(times_transposed(grad_rows, weight_in).astype(jnp.bfloat...]
    all_gather x2 -> x0, waiting for transfers between devices: 108 us -> none  [the longest x1 59.2 us: shards(): lax.all_gather(grad_out, 'col', axis=0, tiled=True)]
    pallas_call x0 -> x1, Pallas kernels: none -> 99.5 us  [shards(): pl.pallas_call(kernel, out_shape=(like(tokens.shape, BF), like(tokens.sha...]
    all_gather x2 -> x0, blocking collectives: 48.1 us -> none  [the longest x1 24.4 us: shards(): lax.all_gather(hidden_act, 'row', axis=0, tiled=True)]
    dot_general x6 -> x0, matrix products: 23.2 us -> none  [the longest x2 8.76 us: inner_tokens(): lax.dot_general(left, right, (((0,), (0,)), ((), ())), preferred_element_...]
  transfers between devices with their start and end apart: 5 -> 0, of which waited for: 5 -> 0; matrix products, arithmetic and copies ran while one was open for 5% -> 0% of each run, Pallas kernels for 0% -> 0%
where the time goes in v1:
time: 107 us; the launch traced here: 106 us
  Pallas kernels  99.5 us (93%)
  local copies, waits for them, and re-layouts  5.64 us (5%)
    pallas_call x1, Pallas kernels, shards(): pl.pallas_call(kernel, out_shape=(like(tokens.shape, BF), like(tokens.sha...  99.5 us
    unnamed x8, local copies, waits for them, and re-layouts  5.64 us

profile of v1, /device:TPU:1, one launch (start us, length us, event | category | flops | bytes accessed | tf_op | source)
XLA Modules:
  0.0 105.8 jit_solution(16275434708934309385)
XLA Ops:
  0.6 0.0 copy-start
  0.6 0.8 copy-done
  1.4 0.0 copy-start.1
  1.4 0.8 copy-done.1
  2.2 99.5 %block.1 = (bf16[16,1536]{1,0:T(8,128)(2,1)S(1)}, bf16[16,1536]{1,0:T(8,128)(2,1)S(1)}, bf16[1536,768]{1,0:T(8,128)(2,1)S(1)}, bf16[768,1536]{1,0:T(8,128)(2,1)S(1)}) custom-call(bf16[16,1536]{1,0:T(8,128)(2,1)S(1)} %copy-done, bf16[16,1536]{1,0:T(8,128)(2,1)S(1)} %copy-done.1, bf16[1536,768]{1,0:T(8,128)(2,1)} %weight_in.1, bf16[768,1536]{1,0:T(8,128)(2,1)} %weight_out.1), custom_call_target="tpu_custom_call" | custom-call | tf_op jit(solution)/shard_map/block/pallas_call | solution.py:308
  101.7 0.6 copy.12
  102.3 0.6 copy.13
  103.0 1.4 %copy.14 = bf16[1536,768]{1,0:T(8,128)(2,1)} copy(bf16[1536,768]{1,0:T(8,128)(2,1)S(1)} %get-tuple-element.10) | data formatting | bytes 4718592
  104.4 1.4 %copy.15 = bf16[768,1536]{1,0:T(8,128)(2,1)} copy(bf16[768,1536]{1,0:T(8,128)(2,1)S(1)} %get-tuple-element.11) | data formatting | bytes 4718592
Async XLA Ops:
  0.6 0.8 copy-start
  1.4 0.8 copy-start.1

commit v2 on v0

v2 whole, which is shorter than its diff:
```python
import math

import jax
import jax.numpy as jnp
from jax import lax
from jax.experimental import pallas as pl
from jax.experimental.pallas import tpu as pltpu
from jax.sharding import PartitionSpec as P

root_two_pi = math.sqrt(2.0 / math.pi)
BF = jnp.bfloat16
F32 = jnp.float32
NT = (((1,), (1,)), ((), ()))
TN = (((0,), (0,)), ((), ()))
AWAY = (1, 3, 2)
TILE = 256
CHUNKS = (0, 1, 3, 2)
STEPS = (
    ("A0", 0), ("A0", 1), ("A2", 0, 3, 0), ("A2", 0, 1, 0), ("A2", 0, 2, 0), ("A1", 0, 3),
    ("A1", 0, 1), ("A2", 1, 1, 0), ("A2", 1, 3, 0), ("c", 0, 0), ("A2", 1, 2, 0), ("A2", 0, 3, 3),
    ("A2", 0, 1, 3), ("A1", 0, 2), ("c", 0, 1), ("A1", 1, 1), ("A1", 1, 3), ("A2", 0, 2, 3),
    ("A2", 0, 3, 1), ("A2", 0, 1, 1), ("c", 2, 0), ("A2", 0, 2, 1), ("A2", 0, 1, 2),
    ("A2", 0, 3, 2), ("s", 0, 0), ("A1", 1, 2), ("c", 1, 0), ("A2", 0, 2, 2), ("A2", 1, 1, 1),
    ("A2", 1, 3, 1), ("s", 0, 1), ("b", 0, 0), ("c", 3, 0), ("A2", 1, 1, 3), ("A2", 1, 2, 1),
    ("A2", 1, 3, 3), ("s", 2, 0), ("b", 0, 1), ("p", 0, 0), ("A2", 1, 2, 3), ("c", 1, 1),
    ("A2", 1, 1, 2), ("A2", 1, 3, 2), ("s", 1, 0), ("b", 2, 0), ("c", 2, 1), ("A2", 1, 2, 2),
    ("p", 0, 1), ("s", 3, 0), ("b", 1, 0), ("c", 3, 1), ("p", 2, 0), ("g", 0, 0), ("b", 3, 0),
    ("p", 1, 0), ("s", 1, 1), ("h", 0, 0), ("p", 3, 0), ("s", 2, 1), ("b", 1, 1), ("g", 0, 1),
    ("p", 1, 1), ("b", 2, 1), ("X", 0, 0), ("s", 3, 1), ("h", 0, 1), ("p", 2, 1), ("g", 2, 0),
    ("b", 3, 1), ("g", 1, 0), ("X", 0, 1), ("h", 2, 0), ("p", 3, 1), ("g", 3, 0), ("h", 1, 0),
    ("WO", 0), ("g", 1, 1), ("h", 3, 0), ("X", 2, 0), ("WO", 1), ("g", 2, 1), ("X", 1, 0),
    ("h", 1, 1), ("g", 3, 1), ("h", 2, 1), ("X", 3, 0), ("WI", 0), ("WI", 1), ("h", 3, 1),
    ("WO", 2), ("X", 1, 1), ("WI", 2), ("WI", 3), ("WI", 4), ("X", 2, 1), ("WI", 5), ("Z", 0),
    ("X", 3, 1), ("Z", 1),
)


def gelu_pair(pre):
    inner = root_two_pi * (pre + 0.044715 * pre * pre * pre)
    bent = jnp.tanh(inner)
    act = 0.5 * pre * (1.0 + bent)
    slope = 0.5 * (1.0 + bent) + 0.5 * pre * (1.0 - bent * bent) * root_two_pi * (
        1.0 + 3.0 * 0.044715 * pre * pre
    )
    return act, slope


def kernel(
    tokens, grad_out, weight_in, weight_out,
    output, grad_in, grad_w_in, grad_w_out,
    panel, w_in, w_out, part, y_recv, z_send, z_own, z_recv, slope, hidden,
    o_part, o_recv, x_send, x_recv, e_send, e_recv, final, gw_in, gw_out,
    load_sem, store_sem, gi_sem, go_sem,
    az_rs, az_ss, ax_rs, ax_ss, sib_rs, sib_ss,
    y_rs, y_ss, z_rs, z_ss, p_rs, p_ss, hy_rs, hy_ss,
    o_rs, o_ss, x_rs, x_ss, e_rs, e_ss,
):
    row, col = lax.axis_index("row"), lax.axis_index("col")
    y, low = lax.rem(row, 4), lax.div(row, 4)
    core, x, z = lax.rem(col, 2), lax.rem(lax.div(col, 2), 4), lax.div(col, 8)

    def around(place, step):
        return lax.rem(place + step, 4)

    sibling = (row, z * 8 + x * 2 + (1 - core))
    partner = ((1 - low) * 4 + y, col)
    x_peer = {d: (row, z * 8 + around(x, d) * 2 + core) for d in AWAY}
    z_peer = {d: (row, around(z, d) * 8 + x * 2 + core) for d in AWAY}
    y_peer = {d: (low * 4 + around(y, d), col) for d in AWAY}
    sends = []

    def send(src, dst, send_sem, recv_sem, device):
        copy = pltpu.make_async_remote_copy(
            src_ref=src, dst_ref=dst, send_sem=send_sem, recv_sem=recv_sem,
            device_id=device, device_id_type=pl.DeviceIdType.MESH,
        )
        copy.start()
        sends.append(copy)

    def arrived(dst, send_sem, recv_sem):
        pltpu.make_async_remote_copy(
            src_ref=dst, dst_ref=dst, send_sem=send_sem, recv_sem=recv_sem,
            device_id=sibling, device_id_type=pl.DeviceIdType.MESH,
        ).wait_recv()

    loads = [
        pltpu.make_async_copy(tokens, panel.at[0, z, core, x], load_sem.at[0]),
        pltpu.make_async_copy(grad_out, panel.at[1, z, core, x], load_sem.at[1]),
        pltpu.make_async_copy(weight_in, w_in, load_sem.at[2]),
        pltpu.make_async_copy(weight_out, w_out, load_sem.at[3]),
    ]
    for load in loads:
        load.start()
    peers = [sibling, partner] + [p[d] for p in (x_peer, z_peer, y_peer) for d in AWAY]
    barrier = pltpu.get_barrier_semaphore()
    for peer in peers:
        pl.semaphore_signal(barrier, inc=1, device_id=peer, device_id_type=pl.DeviceIdType.MESH)
    pl.semaphore_wait(barrier, len(peers))

    def block(a, dx, dz, c):
        return panel.at[a, around(z, dz), c, around(x, dx)]

    def to_sibling(a, dx, dz):
        mine = block(a, dx, dz, core)
        send(mine, mine, sib_ss.at[a, dx, dz], sib_rs.at[a, dx, dz], sibling)

    def along_x(a, dz):
        mine = block(a, 0, dz, core)
        for d in AWAY:
            send(mine, mine, ax_ss.at[a, d, dz], ax_rs.at[a, 4 - d, dz], x_peer[d])

    def gather_own(a):
        loads[a].wait()
        along_x(a, 0)
        mine = block(a, 0, 0, core)
        for d in AWAY:
            send(mine, mine, az_ss.at[a, d], az_rs.at[a, 4 - d], z_peer[d])
        to_sibling(a, 0, 0)

    def gather_z(a, dz):
        arrived(block(a, 0, dz, core), az_ss.at[a, dz], az_rs.at[a, dz])
        along_x(a, dz)
        to_sibling(a, 0, dz)

    def gather_x(a, dx, dz):
        arrived(block(a, dx, dz, core), ax_ss.at[a, dx, dz], ax_rs.at[a, dx, dz])
        to_sibling(a, dx, dz)

    ready = set()

    def first(i, a):
        dz = CHUNKS[i]
        zk = around(z, dz)
        for dx in range(4):
            arrived(block(a, dx, dz, 1 - core), sib_ss.at[a, dx, dz], sib_rs.at[a, dx, dz])
        if a not in ready:
            ready.add(a)
            loads[2 + a].wait()

        @pl.loop(0, 768 // TILE)
        def _(n):
            cols = pl.ds(pl.multiple_of(n * TILE, TILE), TILE)
            left = panel[a, zk].reshape(128, 1536)
            if a == 0:
                total = jnp.dot(left, w_in[:, cols], preferred_element_type=F32)
            else:
                total = lax.dot_general(left, w_out[cols, :], NT, preferred_element_type=F32)
            part[i, a, :, :, :, cols] = total.astype(BF).reshape(4, 2, 16, TILE)

        for d in AWAY:
            send(
                part.at[i, a, around(y, d)], y_recv.at[i, a, 3 - d],
                y_ss.at[i, a, d - 1], y_rs.at[i, a, 3 - d], y_peer[d],
            )

    def sum_y(i, a):
        for d in AWAY:
            arrived(y_recv.at[i, a, d - 1], y_ss.at[i, a, d - 1], y_rs.at[i, a, d - 1])

        def total(which):
            t = part[i, a, y, which].astype(F32)
            for j in range(3):
                t = t + y_recv[i, a, j, which].astype(F32)
            return t

        z_send[i, a] = total(1 - low).astype(BF)
        send(z_send.at[i, a], z_recv.at[i, a], z_ss.at[i, a], z_rs.at[i, a], partner)
        z_own[i, a] = total(low)

    def bend(i, a):
        zk = around(z, CHUNKS[i])
        arrived(z_recv.at[i, a], z_ss.at[i, a], z_rs.at[i, a])
        total = z_own[i, a] + z_recv[i, a].astype(F32)
        if a == 0:
            act, bent = gelu_pair(total)
            slope[i] = bent
            hidden[a, zk, y, low] = act.astype(BF)
        else:
            hidden[a, zk, y, low] = (total * slope[i]).astype(BF)
        mine = hidden.at[a, zk, y, low]
        send(mine, mine, p_ss.at[i, a], p_rs.at[i, a], partner)

    def pass_on(i, a):
        zk = around(z, CHUNKS[i])
        arrived(hidden.at[a, zk, y, 1 - low], p_ss.at[i, a], p_rs.at[i, a])
        both = hidden.at[a, zk, y]
        for d in AWAY:
            send(both, both, hy_ss.at[i, a, d - 1], hy_rs.at[i, a, 3 - d], y_peer[d])

    def second(i, a):
        zk = around(z, CHUNKS[i])
        for d in AWAY:
            both = hidden.at[a, zk, around(y, d)]
            arrived(both, hy_ss.at[i, a, d - 1], hy_rs.at[i, a, d - 1])

        @pl.loop(0, 1536 // TILE)
        def _(n):
            cols = pl.ds(pl.multiple_of(n * TILE, TILE), TILE)
            left = hidden[a, zk].reshape(128, 768)
            if a == 0:
                total = jnp.dot(left, w_out[:, cols], preferred_element_type=F32)
            else:
                total = lax.dot_general(left, w_in[cols, :], NT, preferred_element_type=F32)
            o_part[i, a, :, :, :, cols] = total.astype(BF).reshape(2, 4, 16, TILE)

        send(
            o_part.at[i, a, 1 - core], o_recv.at[i, a], o_ss.at[i, a], o_rs.at[i, a], sibling
        )

    def sum_core(i, a):
        arrived(o_recv.at[i, a], o_ss.at[i, a], o_rs.at[i, a])
        for d in (2, 1, 3, 0):
            xk = around(x, d)
            total = o_part[i, a, core, xk].astype(F32) + o_recv[i, a, xk].astype(F32)
            x_send[i, a, d] = total.astype(BF)
            if d > 0:
                send(
                    x_send.at[i, a, d], x_recv.at[i, a, 3 - d],
                    x_ss.at[i, a, d - 1], x_rs.at[i, a, 3 - d], x_peer[d],
                )

    def sum_x(i, a):
        for d in AWAY:
            arrived(x_recv.at[i, a, d - 1], x_ss.at[i, a, d - 1], x_rs.at[i, a, d - 1])
        total = x_send[i, a, 0].astype(F32)
        for j in range(3):
            total = total + x_recv[i, a, j].astype(F32)
        e_send[i, a] = total.astype(BF)
        dz = CHUNKS[i]
        if dz > 0:
            send(
                e_send.at[i, a], e_recv.at[a, 3 - dz],
                e_ss.at[a, dz - 1], e_rs.at[a, 3 - dz], z_peer[dz],
            )

    stores = []

    def sum_z(a):
        for d in AWAY:
            arrived(e_recv.at[a, d - 1], e_ss.at[a, d - 1], e_rs.at[a, d - 1])
        total = e_send[CHUNKS.index(0), a].astype(F32)
        for j in range(3):
            total = total + e_recv[a, j].astype(F32)
        final[a] = total.astype(BF)
        store = pltpu.make_async_copy(final.at[a], (output, grad_in)[a], store_sem.at[a])
        store.start()
        stores.append(store)

    factor = 1.0 / math.sqrt(512)

    def weight_in_grad(m):
        cols = pl.ds(m * TILE, TILE)
        left = panel[0, :, :, :, :, cols].reshape(512, TILE)
        grad = lax.dot_general(left, hidden[1].reshape(512, 768), TN, preferred_element_type=F32)
        gw_in[cols, :] = (grad * factor).astype(BF)
        store = pltpu.make_async_copy(gw_in.at[cols], grad_w_in.at[cols], gi_sem.at[m])
        store.start()
        stores.append(store)

    def weight_out_grad(m):
        cols = pl.ds(m * TILE, TILE)
        left = hidden[0, :, :, :, :, cols].reshape(512, TILE)
        grad = lax.dot_general(left, panel[1].reshape(512, 1536), TN, preferred_element_type=F32)
        gw_out[cols, :] = (grad * factor).astype(BF)
        store = pltpu.make_async_copy(gw_out.at[cols], grad_w_out.at[cols], go_sem.at[m])
        store.start()
        stores.append(store)

    does = {
        "A0": gather_own, "A1": gather_z, "A2": gather_x, "c": first, "s": sum_y, "b": bend,
        "p": pass_on, "g": second, "h": sum_core, "X": sum_x, "Z": sum_z,
        "WI": weight_in_grad, "WO": weight_out_grad,
    }
    for name, *where in STEPS:
        does[name](*where)
    for store in stores:
        store.wait()
    for copy in sends:
        copy.wait_send()


def shards(tokens, grad_out, weight_in, weight_out):
    dma = pltpu.SemaphoreType.DMA
    vmem = pltpu.VMEM
    like = jax.ShapeDtypeStruct
    return pl.pallas_call(
        kernel,
        out_shape=(
            like(tokens.shape, BF),
            like(tokens.shape, BF),
            like(weight_in.shape, BF),
            like(weight_out.shape, BF),
        ),
        in_specs=[pl.BlockSpec(memory_space=pl.ANY)] * 4,
        out_specs=[pl.BlockSpec(memory_space=pl.ANY)] * 4,
        scratch_shapes=[
            vmem((2, 4, 2, 4, 16, 1536), BF),
            vmem((1536, 768), BF),
            vmem((768, 1536), BF),
            vmem((4, 2, 4, 2, 16, 768), BF),
            vmem((4, 2, 3, 2, 16, 768), BF),
            vmem((4, 2, 16, 768), BF),
            vmem((4, 2, 16, 768), F32),
            vmem((4, 2, 16, 768), BF),
            vmem((4, 16, 768), F32),
            vmem((2, 4, 4, 2, 16, 768), BF),
            vmem((4, 2, 2, 4, 16, 1536), BF),
            vmem((4, 2, 4, 16, 1536), BF),
            vmem((4, 2, 4, 16, 1536), BF),
            vmem((4, 2, 3, 16, 1536), BF),
            vmem((4, 2, 16, 1536), BF),
            vmem((2, 3, 16, 1536), BF),
            vmem((2, 16, 1536), BF),
            vmem((1536, 768), BF),
            vmem((768, 1536), BF),
            dma((4,)), dma((2,)), dma((6,)), dma((3,)),
            dma((2, 4)), dma((2, 4)), dma((2, 4, 4)), dma((2, 4, 4)), dma((2, 4, 4)), dma((2, 4, 4)),
            dma((4, 2, 3)), dma((4, 2, 3)), dma((4, 2)), dma((4, 2)), dma((4, 2)), dma((4, 2)),
            dma((4, 2, 3)), dma((4, 2, 3)),
            dma((4, 2)), dma((4, 2)), dma((4, 2, 3)), dma((4, 2, 3)), dma((2, 3)), dma((2, 3)),
        ],
        compiler_params=pltpu.CompilerParams(
            collective_id=0, has_side_effects=True, vmem_limit_bytes=VMEM_LIMIT
        ),
        name="block",
    )(tokens, grad_out, weight_in, weight_out)


VMEM_LIMIT = 60 * 2**20


def solution(mesh):
    placed = (P("col", "row"), P("col", "row"), P("row", "col"), P("col", "row"))
    return jax.shard_map(
        shards, mesh=mesh, in_specs=placed, out_specs=placed, check_vma=False
    )
```

time: 393 us -> 83.6 us (0.21)
  waiting for transfers between devices: 298 us -> 0 us
  Pallas kernels: 0 us -> 74.9 us
  blocking collectives: 48.1 us -> 0 us
  matrix products: 23.2 us -> 0 us
  between operations: 13.8 us -> 0.64 us
    reduce_scatter x3 -> x0, waiting for transfers between devices: 189 us -> none  [the longest x1 92.1 us: shards(): lax.psum_scatter(times_transposed(grad_rows, weight_in).astype(jnp.bfloat...]
    all_gather x2 -> x0, waiting for transfers between devices: 108 us -> none  [the longest x1 59.2 us: shards(): lax.all_gather(grad_out, 'col', axis=0, tiled=True)]
    pallas_call x0 -> x1, Pallas kernels: none -> 74.9 us  [shards(): pl.pallas_call(kernel, out_shape=(like(tokens.shape, BF), like(tokens.sha...]
    all_gather x2 -> x0, blocking collectives: 48.1 us -> none  [the longest x1 24.4 us: shards(): lax.all_gather(hidden_act, 'row', axis=0, tiled=True)]
    dot_general x6 -> x0, matrix products: 23.2 us -> none  [the longest x2 8.76 us: inner_tokens(): lax.dot_general(left, right, (((0,), (0,)), ((), ())), preferred_element_...]
  transfers between devices with their start and end apart: 5 -> 0, of which waited for: 5 -> 0; matrix products, arithmetic and copies ran while one was open for 5% -> 0% of each run, Pallas kernels for 0% -> 0%
where the time goes in v2:
time: 83.6 us; the launch traced here: 83.1 us
  Pallas kernels  74.9 us (90%)
  local copies, waits for them, and re-layouts  7.62 us (9%)
    pallas_call x1, Pallas kernels, shards(): pl.pallas_call(kernel, out_shape=(like(tokens.shape, BF), like(tokens.sha...  74.9 us
    unnamed x6, local copies, waits for them, and re-layouts  7.62 us

profile of v2, /device:TPU:1, one launch (start us, length us, event | category | flops | bytes accessed | tf_op | source)
XLA Modules:
  0.0 83.1 jit_solution(11842680505166015247)
XLA Ops:
  0.6 74.9 %block.1 = (bf16[16,1536]{1,0:T(8,128)(2,1)}, bf16[16,1536]{1,0:T(8,128)(2,1)}, bf16[1536,768]{1,0:T(8,128)(2,1)}, bf16[768,1536]{1,0:T(8,128)(2,1)}) custom-call(bf16[16,1536]{1,0:T(8,128)(2,1)} %tokens.1, bf16[16,1536]{1,0:T(8,128)(2,1)} %grad_out.1, bf16[1536,768]{1,0:T(8,128)(2,1)} %weight_in.1, bf16[768,1536]{1,0:T(8,128)(2,1)} %weight_out.1), custom_call_target="tpu_custom_call" | custom-call | tf_op jit(solution)/shard_map/block/pallas_call | solution.py:286
  75.5 1.4 %copy.12 = bf16[16,1536]{1,0:T(8,128)(2,1)} copy(bf16[16,1536]{1,0:T(8,128)(2,1)} %get-tuple-element.8) | data formatting | bytes 98304
  76.9 1.4 %copy.13 = bf16[16,1536]{1,0:T(8,128)(2,1)} copy(bf16[16,1536]{1,0:T(8,128)(2,1)} %get-tuple-element.9) | data formatting | bytes 98304
  78.4 0.0 copy-start
  78.4 3.4 %copy.14 = bf16[1536,768]{1,0:T(8,128)(2,1)} copy(bf16[1536,768]{1,0:T(8,128)(2,1)} %get-tuple-element.10) | data formatting | bytes 4718592
  81.7 0.0 copy-done
  81.7 1.4 %copy.15 = bf16[768,1536]{1,0:T(8,128)(2,1)} copy(bf16[768,1536]{1,0:T(8,128)(2,1)S(1)} %copy-done) | data formatting | bytes 4718592
Async XLA Ops:
  78.4 3.4 %copy-start = (bf16[768,1536]{1,0:T(8,128)(2,1)S(1)}, bf16[768,1536]{1,0:T(8,128)(2,1)}, u32[]{:S(2)}) copy-start(bf16[768,1536]{1,0:T(8,128)(2,1)} %get-tuple-element.11) | copy-start | bytes 7077892

commit v3 on v2

v3 whole, which is shorter than its diff:
```python
import math

import jax
import jax.numpy as jnp
from jax import lax
from jax.experimental import pallas as pl
from jax.experimental.pallas import tpu as pltpu
from jax.sharding import PartitionSpec as P

root_two_pi = math.sqrt(2.0 / math.pi)
BF = jnp.bfloat16
F32 = jnp.float32
NT = (((1,), (1,)), ((), ()))
TN = (((0,), (0,)), ((), ()))
AWAY = (1, 3, 2)
TILE = 256
CHUNKS = (0, 3, 1, 2)
RELAY_X = ((1, 1), (1, 3))
RELAY_Z = ()
RELAY_Y_SUM = ((1, 1), (2, 1), (3, 0), (3, 1))
RELAY_Y = ((0, 0), (0, 1), (1, 0), (2, 0), (3, 0))
RELAY_X_SUM = ()
ON, BACK = (1, 3), (3, 1)
STEPS = (
    ("A0", 0), ("A0", 1), ("A2", 0, 3, 0), ("A2", 0, 1, 0), ("A2", 0, 2, 0), ("A1", 0, 3),
    ("A1", 0, 1), ("A2", 1, 1, 0), ("A2", 1, 3, 0), ("c", 0, 0), ("A2", 1, 2, 0), ("A2", 0, 3, 3),
    ("A2", 0, 1, 3), ("A1", 0, 2), ("c", 0, 1), ("A1", 1, 1), ("A1", 1, 3), ("A2", 0, 2, 3),
    ("A2", 0, 3, 1), ("A2", 0, 1, 1), ("c", 1, 0), ("A2", 0, 2, 1), ("A2", 0, 3, 2),
    ("A2", 0, 1, 2), ("s", 0, 0), ("A1", 1, 2), ("c", 2, 0), ("A2", 0, 2, 2), ("A2", 1, 1, 1),
    ("A2", 1, 3, 1), ("s", 0, 1), ("A2", 1, 3, 3), ("A2", 1, 1, 3), ("b", 0, 0), ("c", 3, 0),
    ("s", 1, 0), ("A2", 1, 1, 2), ("A2", 1, 3, 2), ("b", 0, 1), ("A2", 1, 2, 2), ("A2", 1, 2, 1),
    ("s", 2, 0), ("f", 0, 0), ("c", 3, 1), ("r", 3, 0), ("A2", 1, 2, 3), ("b", 1, 0), ("c", 2, 1),
    ("f", 0, 1), ("c", 1, 1), ("g", 0, 0), ("r", 3, 1), ("b", 2, 0), ("s", 3, 0), ("r", 2, 1),
    ("h", 0, 0), ("f", 1, 0), ("g", 0, 1), ("r", 1, 1), ("b", 3, 0), ("s", 3, 1), ("f", 2, 0),
    ("h", 0, 1), ("g", 1, 0), ("s", 2, 1), ("f", 3, 0), ("X", 0, 0), ("s", 1, 1), ("b", 3, 1),
    ("g", 2, 0), ("h", 1, 0), ("b", 2, 1), ("g", 3, 0), ("b", 1, 1), ("h", 2, 0), ("WO", 0),
    ("h", 3, 0), ("g", 3, 1), ("WO", 1), ("g", 2, 1), ("h", 3, 1), ("X", 2, 0), ("g", 1, 1),
    ("h", 2, 1), ("X", 3, 0), ("WO", 2), ("X", 1, 0), ("h", 1, 1), ("WI", 0), ("X", 3, 1),
    ("WI", 1), ("WI", 2), ("WI", 3), ("X", 2, 1), ("WI", 4), ("WI", 5), ("X", 1, 1), ("X", 0, 1),
    ("Z", 0), ("Z", 1),
)


def gelu_pair(pre):
    inner = root_two_pi * (pre + 0.044715 * pre * pre * pre)
    bent = jnp.tanh(inner)
    act = 0.5 * pre * (1.0 + bent)
    slope = 0.5 * (1.0 + bent) + 0.5 * pre * (1.0 - bent * bent) * root_two_pi * (
        1.0 + 3.0 * 0.044715 * pre * pre
    )
    return act, slope


def kernel(
    tokens, grad_out, weight_in, weight_out,
    output, grad_in, grad_w_in, grad_w_out,
    panel, w_in, w_out, part, y_join, y_recv, z_send, z_recv, slope, hidden,
    o_part, o_recv, x_send, x_join, x_recv, e_send, e_recv, load_sem,
    az_rs, az_ss, ax_rs, ax_ss, sib_rs, sib_ss,
    y_rs, y_ss, z_rs, z_ss, hy_rs, hy_ss,
    o_rs, o_ss, x_rs, x_ss, e_rs, e_ss,
):
    row, col = lax.axis_index("row"), lax.axis_index("col")
    y, low = lax.rem(row, 4), lax.div(row, 4)
    core, x, z = lax.rem(col, 2), lax.rem(lax.div(col, 2), 4), lax.div(col, 8)

    def around(place, step):
        return lax.rem(place + step, 4)

    sibling = (row, z * 8 + x * 2 + (1 - core))
    partner = ((1 - low) * 4 + y, col)
    x_peer = {d: (row, z * 8 + around(x, d) * 2 + core) for d in AWAY}
    z_peer = {d: (row, around(z, d) * 8 + x * 2 + core) for d in AWAY}
    y_peer = {d: (low * 4 + around(y, d), col) for d in AWAY}
    sends = []

    def send(src, dst, send_sem, recv_sem, device):
        copy = pltpu.make_async_remote_copy(
            src_ref=src, dst_ref=dst, send_sem=send_sem, recv_sem=recv_sem,
            device_id=device, device_id_type=pl.DeviceIdType.MESH,
        )
        copy.start()
        sends.append(copy)

    def arrived(dst, send_sem, recv_sem):
        pltpu.make_async_remote_copy(
            src_ref=dst, dst_ref=dst, send_sem=send_sem, recv_sem=recv_sem,
            device_id=sibling, device_id_type=pl.DeviceIdType.MESH,
        ).wait_recv()

    loads = [
        pltpu.make_async_copy(tokens, panel.at[0, z, core, x], load_sem.at[0]),
        pltpu.make_async_copy(grad_out, panel.at[1, z, core, x], load_sem.at[1]),
        pltpu.make_async_copy(weight_in, w_in, load_sem.at[2]),
        pltpu.make_async_copy(weight_out, w_out, load_sem.at[3]),
    ]
    for load in loads:
        load.start()
    peers = [sibling, partner] + [p[d] for p in (x_peer, z_peer, y_peer) for d in AWAY]
    barrier = pltpu.get_barrier_semaphore()
    for peer in peers:
        pl.semaphore_signal(barrier, inc=1, device_id=peer, device_id_type=pl.DeviceIdType.MESH)
    pl.semaphore_wait(barrier, len(peers))

    def block(a, dx, dz, c):
        return panel.at[a, around(z, dz), c, around(x, dx)]

    def to_sibling(a, dx, dz):
        mine = block(a, dx, dz, core)
        send(mine, mine, sib_ss.at[a, dx, dz], sib_rs.at[a, dx, dz], sibling)

    def along_x(a, dz):
        mine = block(a, 0, dz, core)
        for d in AWAY[:2] if (a, dz) in RELAY_X else AWAY:
            send(mine, mine, ax_ss.at[a, d, dz], ax_rs.at[a, 4 - d, dz], x_peer[d])

    def gather_own(a):
        loads[a].wait()
        along_x(a, 0)
        mine = block(a, 0, 0, core)
        for d in AWAY[:2] if a in RELAY_Z else AWAY:
            send(mine, mine, az_ss.at[a, d], az_rs.at[a, 4 - d], z_peer[d])
        to_sibling(a, 0, 0)

    def gather_z(a, dz):
        arrived(block(a, 0, dz, core), az_ss.at[a, dz], az_rs.at[a, dz])
        along_x(a, dz)
        if a in RELAY_Z and dz == BACK[a]:
            mine = block(a, 0, dz, core)
            send(mine, mine, az_ss.at[a, 2], az_rs.at[a, 2], z_peer[ON[a]])
        to_sibling(a, 0, dz)

    def gather_x(a, dx, dz):
        arrived(block(a, dx, dz, core), ax_ss.at[a, dx, dz], ax_rs.at[a, dx, dz])
        if (a, dz) in RELAY_X and dx == BACK[a]:
            mine = block(a, dx, dz, core)
            send(mine, mine, ax_ss.at[a, 2, dz], ax_rs.at[a, 2, dz], x_peer[ON[a]])
        to_sibling(a, dx, dz)

    ready = set()

    def first(i, a):
        dz = CHUNKS[i]
        zk = around(z, dz)
        for dx in range(4):
            arrived(block(a, dx, dz, 1 - core), sib_ss.at[a, dx, dz], sib_rs.at[a, dx, dz])
        if a not in ready:
            ready.add(a)
            loads[2 + a].wait()

        @pl.loop(0, 768 // TILE)
        def _(n):
            cols = pl.ds(pl.multiple_of(n * TILE, TILE), TILE)
            left = panel[a, zk].reshape(128, 1536)
            if a == 0:
                total = jnp.dot(left, w_in[:, cols], preferred_element_type=F32)
            else:
                total = lax.dot_general(left, w_out[cols, :], NT, preferred_element_type=F32)
            part[i, a, :, :, :, cols] = total.astype(BF).reshape(4, 2, 16, TILE)

        def to_y(d, slot, device):
            send(
                part.at[i, a, around(y, d)], y_recv.at[i, a, slot],
                y_ss.at[i, a, slot], y_rs.at[i, a, slot], y_peer[device],
            )

        if (i, a) in RELAY_Y_SUM:
            to_y(2, 0, ON[a])
            to_y(BACK[a], 1, BACK[a])
        else:
            for d in AWAY:
                to_y(d, 3 - d, d)

    def y_arrived(i, a, slot):
        arrived(y_recv.at[i, a, slot], y_ss.at[i, a, slot], y_rs.at[i, a, slot])

    def join_y(i, a):
        y_arrived(i, a, 0)
        total = part[i, a, around(y, ON[a])].astype(F32) + y_recv[i, a, 0].astype(F32)
        y_join[i, a] = total.astype(BF)
        send(
            y_join.at[i, a], y_recv.at[i, a, 2],
            y_ss.at[i, a, 2], y_rs.at[i, a, 2], y_peer[ON[a]],
        )

    def sum_y(i, a):
        slots = (1, 2) if (i, a) in RELAY_Y_SUM else (0, 1, 2)
        total = part[i, a, y].astype(F32)
        for slot in slots:
            y_arrived(i, a, slot)
        for slot in slots:
            total = total + y_recv[i, a, slot].astype(F32)
        z_send[i, a] = total.astype(BF)
        send(z_send.at[i, a], z_recv.at[i, a], z_ss.at[i, a], z_rs.at[i, a], partner)

    def bend(i, a):
        zk = around(z, CHUNKS[i])
        arrived(z_recv.at[i, a], z_ss.at[i, a], z_rs.at[i, a])
        total = z_send[i, a].astype(F32) + z_recv[i, a].astype(F32)
        if a == 0:
            act, bent = gelu_pair(total)
            slope[i] = bent
            hidden[a, zk, y] = act.astype(BF)
        else:
            hidden[a, zk, y] = (total * slope[i]).astype(BF)
        both = hidden.at[a, zk, y]
        for d in AWAY[:2] if (i, a) in RELAY_Y else AWAY:
            send(both, both, hy_ss.at[i, a, d - 1], hy_rs.at[i, a, 3 - d], y_peer[d])

    def hidden_arrived(i, a, d):
        both = hidden.at[a, around(z, CHUNKS[i]), around(y, d)]
        arrived(both, hy_ss.at[i, a, d - 1], hy_rs.at[i, a, d - 1])
        return both

    def pass_on(i, a):
        both = hidden_arrived(i, a, BACK[a])
        send(both, both, hy_ss.at[i, a, 1], hy_rs.at[i, a, 1], y_peer[ON[a]])

    def second(i, a):
        zk = around(z, CHUNKS[i])
        for d in (ON[a], 2) if (i, a) in RELAY_Y else AWAY:
            hidden_arrived(i, a, d)

        @pl.loop(0, 1536 // TILE)
        def _(n):
            cols = pl.ds(pl.multiple_of(n * TILE, TILE), TILE)
            left = hidden[a, zk].reshape(128, 768)
            if a == 0:
                total = jnp.dot(left, w_out[:, cols], preferred_element_type=F32)
            else:
                total = lax.dot_general(left, w_in[cols, :], NT, preferred_element_type=F32)
            o_part[i, a, :, :, :, cols] = total.astype(BF).reshape(2, 4, 16, TILE)

        send(
            o_part.at[i, a, 1 - core], o_recv.at[i, a], o_ss.at[i, a], o_rs.at[i, a], sibling
        )

    def to_x(i, a, src, slot, device):
        send(
            src, x_recv.at[i, a, slot], x_ss.at[i, a, slot], x_rs.at[i, a, slot], x_peer[device]
        )

    def x_arrived(i, a, slot):
        arrived(x_recv.at[i, a, slot], x_ss.at[i, a, slot], x_rs.at[i, a, slot])

    def sum_core(i, a):
        arrived(o_recv.at[i, a], o_ss.at[i, a], o_rs.at[i, a])
        relay = (i, a) in RELAY_X_SUM
        for d in (2, BACK[a], ON[a], 0):
            xk = around(x, d)
            total = o_part[i, a, core, xk].astype(F32) + o_recv[i, a, xk].astype(F32)
            x_send[i, a, d] = total.astype(BF)
            if relay and d == 2:
                to_x(i, a, x_send.at[i, a, d], 0, ON[a])
            elif relay and d == BACK[a]:
                to_x(i, a, x_send.at[i, a, d], 1, d)
            elif not relay and d > 0:
                to_x(i, a, x_send.at[i, a, d], 3 - d, d)

    def join_x(i, a):
        x_arrived(i, a, 0)
        total = x_send[i, a, ON[a]].astype(F32) + x_recv[i, a, 0].astype(F32)
        x_join[i, a] = total.astype(BF)
        to_x(i, a, x_join.at[i, a], 2, ON[a])

    def sum_x(i, a):
        slots = (1, 2) if (i, a) in RELAY_X_SUM else (0, 1, 2)
        for slot in slots:
            x_arrived(i, a, slot)
        total = x_send[i, a, 0].astype(F32)
        for slot in slots:
            total = total + x_recv[i, a, slot].astype(F32)
        e_send[i, a] = total.astype(BF)
        dz = CHUNKS[i]
        if dz > 0:
            send(
                e_send.at[i, a], e_recv.at[a, 3 - dz],
                e_ss.at[a, dz - 1], e_rs.at[a, 3 - dz], z_peer[dz],
            )

    def sum_z(a):
        for d in AWAY:
            arrived(e_recv.at[a, d - 1], e_ss.at[a, d - 1], e_rs.at[a, d - 1])
        total = e_send[CHUNKS.index(0), a].astype(F32)
        for j in range(3):
            total = total + e_recv[a, j].astype(F32)
        (output, grad_in)[a][...] = total.astype(BF)

    factor = 1.0 / math.sqrt(512)

    def weight_in_grad(m):
        cols = pl.ds(m * TILE, TILE)
        left = panel[0, :, :, :, :, cols].reshape(512, TILE)
        grad = lax.dot_general(left, hidden[1].reshape(512, 768), TN, preferred_element_type=F32)
        grad_w_in[cols, :] = (grad * factor).astype(BF)

    def weight_out_grad(m):
        cols = pl.ds(m * TILE, TILE)
        left = hidden[0, :, :, :, :, cols].reshape(512, TILE)
        grad = lax.dot_general(left, panel[1].reshape(512, 1536), TN, preferred_element_type=F32)
        grad_w_out[cols, :] = (grad * factor).astype(BF)

    does = {
        "A0": gather_own, "A1": gather_z, "A2": gather_x, "c": first, "s": sum_y, "b": bend,
        "r": join_y, "f": pass_on, "g": second, "h": sum_core, "q": join_x, "X": sum_x, "Z": sum_z,
        "WI": weight_in_grad, "WO": weight_out_grad,
    }
    for name, *where in STEPS:
        does[name](*where)
    for copy in sends:
        copy.wait_send()


def write_out(*refs):
    n = len(refs) // 2
    copies = [pltpu.make_async_copy(refs[j], refs[n + j], refs[-1].at[j]) for j in range(n)]
    for copy in copies:
        copy.start()
    for copy in copies:
        copy.wait()


def shards(tokens, grad_out, weight_in, weight_out):
    dma = pltpu.SemaphoreType.DMA
    vmem = pltpu.VMEM
    like = jax.ShapeDtypeStruct
    shapes = (
        like(tokens.shape, BF), like(tokens.shape, BF),
        like(weight_in.shape, BF), like(weight_out.shape, BF),
    )
    results = pl.pallas_call(
        kernel,
        out_shape=shapes,
        in_specs=[pl.BlockSpec(memory_space=IN_SPACE)] * 4,
        out_specs=[pl.BlockSpec(memory_space=OUT_SPACE)] * 4,
        scratch_shapes=[
            vmem((2, 4, 2, 4, 16, 1536), BF),
            vmem((1536, 768), BF),
            vmem((768, 1536), BF),
            vmem((4, 2, 4, 2, 16, 768), BF),
            vmem((4, 2, 2, 16, 768), BF),
            vmem((4, 2, 3, 2, 16, 768), BF),
            vmem((4, 2, 2, 16, 768), BF),
            vmem((4, 2, 2, 16, 768), BF),
            vmem((4, 2, 16, 768), F32),
            vmem((2, 4, 4, 2, 16, 768), BF),
            vmem((4, 2, 2, 4, 16, 1536), BF),
            vmem((4, 2, 4, 16, 1536), BF),
            vmem((4, 2, 4, 16, 1536), BF),
            vmem((4, 2, 16, 1536), BF),
            vmem((4, 2, 3, 16, 1536), BF),
            vmem((4, 2, 16, 1536), BF),
            vmem((2, 3, 16, 1536), BF),
            dma((4,)),
            dma((2, 4)), dma((2, 4)), dma((2, 4, 4)), dma((2, 4, 4)), dma((2, 4, 4)), dma((2, 4, 4)),
            dma((4, 2, 3)), dma((4, 2, 3)), dma((4, 2)), dma((4, 2)), dma((4, 2, 3)), dma((4, 2, 3)),
            dma((4, 2)), dma((4, 2)), dma((4, 2, 3)), dma((4, 2, 3)), dma((2, 3)), dma((2, 3)),
        ],
        compiler_params=pltpu.CompilerParams(
            collective_id=0, has_side_effects=True, vmem_limit_bytes=VMEM_LIMIT
        ),
        name="block",
    )(tokens, grad_out, weight_in, weight_out)
    return pl.pallas_call(
        write_out,
        out_shape=shapes,
        in_specs=[pl.BlockSpec(memory_space=MID_SPACE)] * 4,
        out_specs=[pl.BlockSpec(memory_space=pl.ANY)] * 4,
        scratch_shapes=[dma((4,))],
        compiler_params=pltpu.CompilerParams(vmem_limit_bytes=2**20),
        name="write_out",
    )(*results)


IN_SPACE = pltpu.HBM
OUT_SPACE = pltpu.VMEM
MID_SPACE = pltpu.VMEM
VMEM_LIMIT = 48 * 2**20


def solution(mesh):
    placed = (P("col", "row"), P("col", "row"), P("row", "col"), P("col", "row"))
    return jax.shard_map(
        shards, mesh=mesh, in_specs=placed, out_specs=placed, check_vma=False
    )
```

time: 83.6 us -> 76.6 us (0.916)
  local copies, waits for them, and re-layouts: 7.62 us -> 1.59 us
  Pallas kernels: 74.9 us -> 73.1 us
    unnamed x6 -> x4, local copies, waits for them, and re-layouts: 7.62 us -> 1.59 us
    pallas_call x1 -> x2, Pallas kernels: 74.9 us -> 73.1 us  [the longest x1 70.8 us: shards(): pl.pallas_call(kernel, out_shape=shapes, in_specs=[pl.BlockSpec(memory_sp...]
where the time goes in v3:
time: 76.6 us; the launch traced here: 75.3 us
  Pallas kernels  73.1 us (95%)
  local copies, waits for them, and re-layouts  1.59 us (2%)
    pallas_call x1, Pallas kernels, shards(): pl.pallas_call(kernel, out_shape=shapes, in_specs=[pl.BlockSpec(memory_sp...  70.8 us
    pallas_call x1, Pallas kernels, shards(): pl.pallas_call(write_out, out_shape=shapes, in_specs=[pl.BlockSpec(memory...  2.25 us
    unnamed x4, local copies, waits for them, and re-layouts  1.59 us

profile of v3, /device:TPU:1, one launch (start us, length us, event | category | flops | bytes accessed | tf_op | source)
XLA Modules:
  0.0 75.3 jit_solution(5936677116036362473)
XLA Ops:
  0.6 0.0 copy-start
  0.6 0.8 %copy-done = bf16[16,1536]{1,0:T(8,128)(2,1)S(1)} copy-done((bf16[16,1536]{1,0:T(8,128)(2,1)S(1)}, bf16[16,1536]{1,0:T(8,128)(2,1)}, u32[]{:S(2)}) %copy-start) | copy-done | bytes 49176
  1.4 0.0 copy-start.1
  1.4 0.8 %copy-done.1 = bf16[16,1536]{1,0:T(8,128)(2,1)S(1)} copy-done((bf16[16,1536]{1,0:T(8,128)(2,1)S(1)}, bf16[16,1536]{1,0:T(8,128)(2,1)}, u32[]{:S(2)}) %copy-start.1) | copy-done | bytes 49176
  2.2 70.8 %block.1 = (bf16[16,1536]{1,0:T(8,128)(2,1)S(1)}, bf16[16,1536]{1,0:T(8,128)(2,1)S(1)}, bf16[1536,768]{1,0:T(8,128)(2,1)S(1)}, bf16[768,1536]{1,0:T(8,128)(2,1)S(1)}) custom-call(bf16[16,1536]{1,0:T(8,128)(2,1)S(1)} %copy-done, bf16[16,1536]{1,0:T(8,128)(2,1)S(1)} %copy-done.1, bf16[1536,768]{1,0:T(8,128)(2,1)} %weight_in.1, bf16[768,1536]{1,0:T(8,128)(2,1)} %weight_out.1), custom_call_target="tpu_custom_call" | custom-call | tf_op jit(solution)/shard_map/block/pallas_call | solution.py:331
  73.1 2.3 %write_out.1 = (bf16[16,1536]{1,0:T(8,128)(2,1)}, bf16[16,1536]{1,0:T(8,128)(2,1)}, bf16[1536,768]{1,0:T(8,128)(2,1)}, bf16[768,1536]{1,0:T(8,128)(2,1)}) custom-call(bf16[16,1536]{1,0:T(8,128)(2,1)S(1)} %get-tuple-element.8.refs_0_, bf16[16,1536]{1,0:T(8,128)(2,1)S(1)} %get-tuple-element.9.refs_1_, bf16[1536,768]{1,0:T(8,128)(2,1)S(1)} %get-tuple-element.10.refs_2_, ...), custom_call_target="tpu_custom_call" | custom-call | tf_op jit(solution)/shard_map/write_out/pallas_call | solution.py:364
Async XLA Ops:
  0.6 0.8 %copy-start = (bf16[16,1536]{1,0:T(8,128)(2,1)S(1)}, bf16[16,1536]{1,0:T(8,128)(2,1)}, u32[]{:S(2)}) copy-start(bf16[16,1536]{1,0:T(8,128)(2,1)} %tokens.1) | copy-start | bytes 147460
  1.4 0.8 %copy-start.1 = (bf16[16,1536]{1,0:T(8,128)(2,1)S(1)}, bf16[16,1536]{1,0:T(8,128)(2,1)}, u32[]{:S(2)}) copy-start(bf16[16,1536]{1,0:T(8,128)(2,1)} %grad_out.1) | copy-start | bytes 147460

commit v4 on v3

--- a/solution.py
+++ b/solution.py
@@ -14,6 +14,8 @@
 TN = (((0,), (0,)), ((), ()))
 AWAY = (1, 3, 2)
 TILE = 256
+TILE_C = 768
+TILE_G = 1536
 CHUNKS = (0, 3, 1, 2)
 RELAY_X = ((1, 1), (1, 3))
 RELAY_Z = ()
@@ -22,22 +24,21 @@
 RELAY_X_SUM = ()
 ON, BACK = (1, 3), (3, 1)
 STEPS = (
-    ("A0", 0), ("A0", 1), ("A2", 0, 3, 0), ("A2", 0, 1, 0), ("A2", 0, 2, 0), ("A1", 0, 3),
-    ("A1", 0, 1), ("A2", 1, 1, 0), ("A2", 1, 3, 0), ("c", 0, 0), ("A2", 1, 2, 0), ("A2", 0, 3, 3),
-    ("A2", 0, 1, 3), ("A1", 0, 2), ("c", 0, 1), ("A1", 1, 1), ("A1", 1, 3), ("A2", 0, 2, 3),
-    ("A2", 0, 3, 1), ("A2", 0, 1, 1), ("c", 1, 0), ("A2", 0, 2, 1), ("A2", 0, 3, 2),
-    ("A2", 0, 1, 2), ("s", 0, 0), ("A1", 1, 2), ("c", 2, 0), ("A2", 0, 2, 2), ("A2", 1, 1, 1),
-    ("A2", 1, 3, 1), ("s", 0, 1), ("A2", 1, 3, 3), ("A2", 1, 1, 3), ("b", 0, 0), ("c", 3, 0),
-    ("s", 1, 0), ("A2", 1, 1, 2), ("A2", 1, 3, 2), ("b", 0, 1), ("A2", 1, 2, 2), ("A2", 1, 2, 1),
-    ("s", 2, 0), ("f", 0, 0), ("c", 3, 1), ("r", 3, 0), ("A2", 1, 2, 3), ("b", 1, 0), ("c", 2, 1),
-    ("f", 0, 1), ("c", 1, 1), ("g", 0, 0), ("r", 3, 1), ("b", 2, 0), ("s", 3, 0), ("r", 2, 1),
-    ("h", 0, 0), ("f", 1, 0), ("g", 0, 1), ("r", 1, 1), ("b", 3, 0), ("s", 3, 1), ("f", 2, 0),
-    ("h", 0, 1), ("g", 1, 0), ("s", 2, 1), ("f", 3, 0), ("X", 0, 0), ("s", 1, 1), ("b", 3, 1),
-    ("g", 2, 0), ("h", 1, 0), ("b", 2, 1), ("g", 3, 0), ("b", 1, 1), ("h", 2, 0), ("WO", 0),
-    ("h", 3, 0), ("g", 3, 1), ("WO", 1), ("g", 2, 1), ("h", 3, 1), ("X", 2, 0), ("g", 1, 1),
-    ("h", 2, 1), ("X", 3, 0), ("WO", 2), ("X", 1, 0), ("h", 1, 1), ("WI", 0), ("X", 3, 1),
-    ("WI", 1), ("WI", 2), ("WI", 3), ("X", 2, 1), ("WI", 4), ("WI", 5), ("X", 1, 1), ("X", 0, 1),
-    ("Z", 0), ("Z", 1),
+    ("A0", 0), ("A0", 1), ("A2", 0, 3, 0), ("A1", 0, 3), ("A2", 0, 2, 0), ("A1", 0, 1),
+    ("A2", 0, 1, 0), ("A2", 1, 1, 0), ("A2", 1, 3, 0), ("c", 0, 0), ("A2", 1, 2, 0), ("A1", 0, 2),
+    ("A2", 0, 3, 3), ("c", 0, 1), ("A2", 0, 1, 3), ("A1", 1, 1), ("A2", 0, 2, 3), ("A2", 0, 3, 1),
+    ("A2", 0, 1, 1), ("c", 1, 0), ("A2", 0, 2, 1), ("A2", 0, 1, 2), ("A1", 1, 2), ("s", 0, 0),
+    ("A2", 0, 3, 2), ("A1", 1, 3), ("c", 2, 0), ("A2", 0, 2, 2), ("A2", 1, 1, 1), ("c", 3, 0),
+    ("b", 0, 0), ("s", 1, 0), ("A2", 1, 3, 2), ("A2", 1, 3, 3), ("A2", 1, 2, 2), ("A2", 1, 1, 3),
+    ("A2", 1, 1, 2), ("A2", 1, 2, 1), ("A2", 1, 3, 1), ("r", 3, 0), ("c", 3, 1), ("s", 2, 0),
+    ("c", 2, 1), ("A2", 1, 2, 3), ("b", 1, 0), ("s", 0, 1), ("c", 1, 1), ("s", 3, 0), ("r", 3, 1),
+    ("r", 2, 1), ("b", 2, 0), ("f", 1, 0), ("r", 1, 1), ("b", 3, 0), ("b", 0, 1), ("s", 3, 1),
+    ("s", 2, 1), ("f", 2, 0), ("g", 1, 0), ("f", 3, 0), ("s", 1, 1), ("b", 3, 1), ("h", 1, 0),
+    ("g", 2, 0), ("b", 2, 1), ("g", 3, 0), ("h", 2, 0), ("b", 1, 1), ("g", 3, 1), ("h", 3, 0),
+    ("f", 0, 1), ("f", 0, 0), ("g", 2, 1), ("h", 3, 1), ("X", 1, 0), ("X", 2, 0), ("g", 1, 1),
+    ("h", 2, 1), ("g", 0, 1), ("g", 0, 0), ("X", 3, 0), ("h", 1, 1), ("X", 3, 1), ("WO", 1),
+    ("WI", 1), ("h", 0, 0), ("WI", 2), ("WI", 5), ("X", 2, 1), ("X", 1, 1), ("h", 0, 1), ("WI", 3),
+    ("WI", 0), ("WO", 0), ("WO", 2), ("WI", 4), ("X", 0, 0), ("Z", 0), ("X", 0, 1), ("Z", 1),
 )
 
 
@@ -148,15 +149,15 @@
             ready.add(a)
             loads[2 + a].wait()
 
-        @pl.loop(0, 768 // TILE)
+        @pl.loop(0, 768 // TILE_C)
         def _(n):
-            cols = pl.ds(pl.multiple_of(n * TILE, TILE), TILE)
+            cols = pl.ds(pl.multiple_of(n * TILE_C, TILE_C), TILE_C)
             left = panel[a, zk].reshape(128, 1536)
             if a == 0:
                 total = jnp.dot(left, w_in[:, cols], preferred_element_type=F32)
             else:
                 total = lax.dot_general(left, w_out[cols, :], NT, preferred_element_type=F32)
-            part[i, a, :, :, :, cols] = total.astype(BF).reshape(4, 2, 16, TILE)
+            part[i, a, :, :, :, cols] = total.astype(BF).reshape(4, 2, 16, TILE_C)
 
         def to_y(d, slot, device):
             send(
@@ -221,15 +222,15 @@
         for d in (ON[a], 2) if (i, a) in RELAY_Y else AWAY:
             hidden_arrived(i, a, d)
 
-        @pl.loop(0, 1536 // TILE)
+        @pl.loop(0, 1536 // TILE_G)
         def _(n):
-            cols = pl.ds(pl.multiple_of(n * TILE, TILE), TILE)
+            cols = pl.ds(pl.multiple_of(n * TILE_G, TILE_G), TILE_G)
             left = hidden[a, zk].reshape(128, 768)
             if a == 0:
                 total = jnp.dot(left, w_out[:, cols], preferred_element_type=F32)
             else:
                 total = lax.dot_general(left, w_in[cols, :], NT, preferred_element_type=F32)
-            o_part[i, a, :, :, :, cols] = total.astype(BF).reshape(2, 4, 16, TILE)
+            o_part[i, a, :, :, :, cols] = total.astype(BF).reshape(2, 4, 16, TILE_G)
 
         send(
             o_part.at[i, a, 1 - core], o_recv.at[i, a], o_ss.at[i, a], o_rs.at[i, a], sibling
@@ -327,6 +328,9 @@
     shapes = (
         like(tokens.shape, BF), like(tokens.shape, BF),
         like(weight_in.shape, BF), like(weight_out.shape, BF),
+    )
+    tokens, grad_out = (
+        pltpu.with_memory_space_constraint(arg, pltpu.HBM) for arg in (tokens, grad_out)
     )
     results = pl.pallas_call(
         kernel,

time: 76.6 us -> 71.8 us (0.937); the launches traced: 75.3 us -> 71.7 us
  Pallas kernels: 73.1 us -> 71.1 us
  local copies, waits for them, and re-layouts: 1.59 us -> 0 us
    pallas_call x1, Pallas kernels: 70.8 us -> 68.8 us  [shards(): pl.pallas_call(kernel, out_shape=shapes, in_specs=[pl.BlockSpec(memory_sp...]
    unnamed x4 -> x0, local copies, waits for them, and re-layouts: 1.59 us -> none
where the time goes in v4:
time: 71.8 us; the launch traced here: 71.7 us
  Pallas kernels  71.1 us (99%)
    pallas_call x1, Pallas kernels, shards(): pl.pallas_call(kernel, out_shape=shapes, in_specs=[pl.BlockSpec(memory_sp...  68.8 us
    pallas_call x1, Pallas kernels, shards(): pl.pallas_call(write_out, out_shape=shapes, in_specs=[pl.BlockSpec(memory...  2.25 us

profile of v4, /device:TPU:1, one launch (start us, length us, event | category | flops | bytes accessed | tf_op | source)
XLA Modules:
  0.0 71.7 jit_solution(9547518955221966422)
XLA Ops:
  0.6 68.8 %block.1 = (bf16[16,1536]{1,0:T(8,128)(2,1)S(1)}, bf16[16,1536]{1,0:T(8,128)(2,1)S(1)}, bf16[1536,768]{1,0:T(8,128)(2,1)S(1)}, bf16[768,1536]{1,0:T(8,128)(2,1)S(1)}) custom-call(bf16[16,1536]{1,0:T(8,128)(2,1)} %tokens.1, bf16[16,1536]{1,0:T(8,128)(2,1)} %grad_out.1, bf16[1536,768]{1,0:T(8,128)(2,1)} %weight_in.1, bf16[768,1536]{1,0:T(8,128)(2,1)} %weight_out.1), custom_call_target="tpu_custom_call" | custom-call | tf_op jit(solution)/shard_map/block/pallas_call | solution.py:335
  69.5 2.3 %write_out.1 = (bf16[16,1536]{1,0:T(8,128)(2,1)}, bf16[16,1536]{1,0:T(8,128)(2,1)}, bf16[1536,768]{1,0:T(8,128)(2,1)}, bf16[768,1536]{1,0:T(8,128)(2,1)}) custom-call(bf16[16,1536]{1,0:T(8,128)(2,1)S(1)} %get-tuple-element.8.refs_0_, bf16[16,1536]{1,0:T(8,128)(2,1)S(1)} %get-tuple-element.9.refs_1_, bf16[1536,768]{1,0:T(8,128)(2,1)S(1)} %get-tuple-element.10.refs_2_, ...), custom_call_target="tpu_custom_call" | custom-call | tf_op jit(solution)/shard_map/write_out/pallas_call | solution.py:368

commit v5 on v4

--- a/solution.py
+++ b/solution.py
@@ -16,29 +16,28 @@
 TILE = 256
 TILE_C = 768
 TILE_G = 1536
-CHUNKS = (0, 3, 1, 2)
-RELAY_X = ((1, 1), (1, 3))
+CHUNKS = (0, 1, 3, 2)
+RELAY_X = ()
 RELAY_Z = ()
-RELAY_Y_SUM = ((1, 1), (2, 1), (3, 0), (3, 1))
-RELAY_Y = ((0, 0), (0, 1), (1, 0), (2, 0), (3, 0))
+RELAY_Y_SUM = ()
+RELAY_Y = ()
 RELAY_X_SUM = ()
 ON, BACK = (1, 3), (3, 1)
 STEPS = (
-    ("A0", 0), ("A0", 1), ("A2", 0, 3, 0), ("A1", 0, 3), ("A2", 0, 2, 0), ("A1", 0, 1),
-    ("A2", 0, 1, 0), ("A2", 1, 1, 0), ("A2", 1, 3, 0), ("c", 0, 0), ("A2", 1, 2, 0), ("A1", 0, 2),
-    ("A2", 0, 3, 3), ("c", 0, 1), ("A2", 0, 1, 3), ("A1", 1, 1), ("A2", 0, 2, 3), ("A2", 0, 3, 1),
-    ("A2", 0, 1, 1), ("c", 1, 0), ("A2", 0, 2, 1), ("A2", 0, 1, 2), ("A1", 1, 2), ("s", 0, 0),
-    ("A2", 0, 3, 2), ("A1", 1, 3), ("c", 2, 0), ("A2", 0, 2, 2), ("A2", 1, 1, 1), ("c", 3, 0),
-    ("b", 0, 0), ("s", 1, 0), ("A2", 1, 3, 2), ("A2", 1, 3, 3), ("A2", 1, 2, 2), ("A2", 1, 1, 3),
-    ("A2", 1, 1, 2), ("A2", 1, 2, 1), ("A2", 1, 3, 1), ("r", 3, 0), ("c", 3, 1), ("s", 2, 0),
-    ("c", 2, 1), ("A2", 1, 2, 3), ("b", 1, 0), ("s", 0, 1), ("c", 1, 1), ("s", 3, 0), ("r", 3, 1),
-    ("r", 2, 1), ("b", 2, 0), ("f", 1, 0), ("r", 1, 1), ("b", 3, 0), ("b", 0, 1), ("s", 3, 1),
-    ("s", 2, 1), ("f", 2, 0), ("g", 1, 0), ("f", 3, 0), ("s", 1, 1), ("b", 3, 1), ("h", 1, 0),
-    ("g", 2, 0), ("b", 2, 1), ("g", 3, 0), ("h", 2, 0), ("b", 1, 1), ("g", 3, 1), ("h", 3, 0),
-    ("f", 0, 1), ("f", 0, 0), ("g", 2, 1), ("h", 3, 1), ("X", 1, 0), ("X", 2, 0), ("g", 1, 1),
-    ("h", 2, 1), ("g", 0, 1), ("g", 0, 0), ("X", 3, 0), ("h", 1, 1), ("X", 3, 1), ("WO", 1),
-    ("WI", 1), ("h", 0, 0), ("WI", 2), ("WI", 5), ("X", 2, 1), ("X", 1, 1), ("h", 0, 1), ("WI", 3),
-    ("WI", 0), ("WO", 0), ("WO", 2), ("WI", 4), ("X", 0, 0), ("Z", 0), ("X", 0, 1), ("Z", 1),
+    ("A0", 0), ("A0", 1), ("A2", 0, 3, 0), ("A2", 0, 1, 0), ("A1", 0, 3), ("A2", 0, 2, 0),
+    ("A2", 1, 3, 0), ("A1", 0, 1), ("c", 0, 0), ("A2", 1, 1, 0), ("A2", 1, 2, 0), ("A2", 0, 1, 3),
+    ("A2", 0, 3, 3), ("A1", 0, 2), ("c", 0, 1), ("A1", 1, 1), ("A2", 0, 2, 3), ("A2", 0, 3, 1),
+    ("A2", 0, 1, 1), ("c", 2, 0), ("A2", 0, 2, 1), ("A1", 1, 2), ("A2", 0, 3, 2), ("A1", 1, 3),
+    ("c", 1, 0), ("A2", 0, 1, 2), ("A2", 0, 2, 2), ("A2", 1, 1, 1), ("c", 3, 0), ("A2", 1, 3, 1),
+    ("A2", 1, 2, 1), ("A2", 1, 1, 2), ("s", 2, 0), ("A2", 1, 3, 2), ("c", 1, 1), ("A2", 1, 2, 2),
+    ("s", 1, 0), ("c", 3, 1), ("A2", 1, 2, 3), ("A2", 1, 3, 3), ("s", 3, 0), ("b", 2, 0),
+    ("s", 0, 1), ("s", 0, 0), ("A2", 1, 1, 3), ("s", 1, 1), ("c", 2, 1), ("b", 3, 0), ("s", 3, 1),
+    ("g", 2, 0), ("b", 1, 0), ("s", 2, 1), ("h", 2, 0), ("b", 1, 1), ("g", 3, 0), ("b", 3, 1),
+    ("b", 2, 1), ("g", 1, 0), ("h", 3, 0), ("b", 0, 0), ("X", 2, 0), ("g", 1, 1), ("h", 1, 0),
+    ("g", 3, 1), ("h", 1, 1), ("b", 0, 1), ("X", 3, 0), ("g", 2, 1), ("h", 3, 1), ("X", 1, 0),
+    ("h", 2, 1), ("g", 0, 0), ("WO", 0), ("X", 1, 1), ("g", 0, 1), ("X", 3, 1), ("h", 0, 0),
+    ("WI", 5), ("h", 0, 1), ("X", 2, 1), ("WI", 1), ("WI", 2), ("WI", 0), ("WO", 2), ("X", 0, 0),
+    ("WO", 1), ("WI", 4), ("Z", 0), ("WI", 3), ("X", 0, 1), ("Z", 1),
 )
 
 
@@ -117,10 +116,10 @@
 
     def gather_own(a):
         loads[a].wait()
-        along_x(a, 0)
         mine = block(a, 0, 0, core)
         for d in AWAY[:2] if a in RELAY_Z else AWAY:
             send(mine, mine, az_ss.at[a, d], az_rs.at[a, 4 - d], z_peer[d])
+        along_x(a, 0)
         to_sibling(a, 0, 0)
 
     def gather_z(a, dz):

time: 71.8 us -> 69.2 us (0.964)
  Pallas kernels: 71.1 us -> 68.2 us
    pallas_call x1, Pallas kernels: 68.8 us -> 66 us  [shards(): pl.pallas_call(kernel, out_shape=shapes, in_specs=[pl.BlockSpec(memory_sp...]
where the time goes in v5:
time: 69.2 us; the launch traced here: 68.9 us
  Pallas kernels  68.2 us (99%)
    pallas_call x1, Pallas kernels, shards(): pl.pallas_call(kernel, out_shape=shapes, in_specs=[pl.BlockSpec(memory_sp...  66 us
    pallas_call x1, Pallas kernels, shards(): pl.pallas_call(write_out, out_shape=shapes, in_specs=[pl.BlockSpec(memory...  2.25 us

profile of v5, /device:TPU:1, one launch (start us, length us, event | category | flops | bytes accessed | tf_op | source)
XLA Modules:
  0.0 68.9 jit_solution(14880842917393828025)
XLA Ops:
  0.6 66.0 %block.1 = (bf16[16,1536]{1,0:T(8,128)(2,1)S(1)}, bf16[16,1536]{1,0:T(8,128)(2,1)S(1)}, bf16[1536,768]{1,0:T(8,128)(2,1)S(1)}, bf16[768,1536]{1,0:T(8,128)(2,1)S(1)}) custom-call(bf16[16,1536]{1,0:T(8,128)(2,1)} %tokens.1, bf16[16,1536]{1,0:T(8,128)(2,1)} %grad_out.1, bf16[1536,768]{1,0:T(8,128)(2,1)} %weight_in.1, bf16[768,1536]{1,0:T(8,128)(2,1)} %weight_out.1), custom_call_target="tpu_custom_call" | custom-call | tf_op jit(solution)/shard_map/block/pallas_call | solution.py:334
  66.6 2.3 %write_out.1 = (bf16[16,1536]{1,0:T(8,128)(2,1)}, bf16[16,1536]{1,0:T(8,128)(2,1)}, bf16[1536,768]{1,0:T(8,128)(2,1)}, bf16[768,1536]{1,0:T(8,128)(2,1)}) custom-call(bf16[16,1536]{1,0:T(8,128)(2,1)S(1)} %get-tuple-element.8.refs_0_, bf16[16,1536]{1,0:T(8,128)(2,1)S(1)} %get-tuple-element.9.refs_1_, bf16[1536,768]{1,0:T(8,128)(2,1)S(1)} %get-tuple-element.10.refs_2_, ...), custom_call_target="tpu_custom_call" | custom-call | tf_op jit(solution)/shard_map/write_out/pallas_call | solution.py:367

commit v6 on v5

--- a/solution.py
+++ b/solution.py
@@ -14,6 +14,7 @@
 TN = (((0,), (0,)), ((), ()))
 AWAY = (1, 3, 2)
 TILE = 256
+LAG = 24
 TILE_C = 768
 TILE_G = 1536
 CHUNKS = (0, 1, 3, 2)
@@ -305,9 +306,16 @@
         "r": join_y, "f": pass_on, "g": second, "h": sum_core, "q": join_x, "X": sum_x, "Z": sum_z,
         "WI": weight_in_grad, "WO": weight_out_grad,
     }
-    for name, *where in STEPS:
+    issued = []
+    waited = 0
+    for step, (name, *where) in enumerate(STEPS):
         does[name](*where)
-    for copy in sends:
+        issued.append(len(sends))
+        if step >= LAG:
+            for copy in sends[waited : issued[step - LAG]]:
+                copy.wait_send()
+            waited = issued[step - LAG]
+    for copy in sends[waited:]:
         copy.wait_send()
 
 

time: 69.2 us -> 69.3 us (level)
  no operation moved by 1% of the time
where the time goes in v6:
time: 69.3 us; the launch traced here: 68.7 us
  Pallas kernels  68.1 us (98%)
    pallas_call x1, Pallas kernels, shards(): pl.pallas_call(kernel, out_shape=shapes, in_specs=[pl.BlockSpec(memory_sp...  65.8 us
    pallas_call x1, Pallas kernels, shards(): pl.pallas_call(write_out, out_shape=shapes, in_specs=[pl.BlockSpec(memory...  2.25 us

profile of v6, /device:TPU:1, one launch (start us, length us, event | category | flops | bytes accessed | tf_op | source)
XLA Modules:
  0.0 68.7 jit_solution(13595738109405196869)
XLA Ops:
  0.6 65.8 %block.1 = (bf16[16,1536]{1,0:T(8,128)(2,1)S(1)}, bf16[16,1536]{1,0:T(8,128)(2,1)S(1)}, bf16[1536,768]{1,0:T(8,128)(2,1)S(1)}, bf16[768,1536]{1,0:T(8,128)(2,1)S(1)}) custom-call(bf16[16,1536]{1,0:T(8,128)(2,1)} %tokens.1, bf16[16,1536]{1,0:T(8,128)(2,1)} %grad_out.1, bf16[1536,768]{1,0:T(8,128)(2,1)} %weight_in.1, bf16[768,1536]{1,0:T(8,128)(2,1)} %weight_out.1), custom_call_target="tpu_custom_call" | custom-call | tf_op jit(solution)/shard_map/block/pallas_call | solution.py:342
  66.4 2.3 %write_out.1 = (bf16[16,1536]{1,0:T(8,128)(2,1)}, bf16[16,1536]{1,0:T(8,128)(2,1)}, bf16[1536,768]{1,0:T(8,128)(2,1)}, bf16[768,1536]{1,0:T(8,128)(2,1)}) custom-call(bf16[16,1536]{1,0:T(8,128)(2,1)S(1)} %get-tuple-element.8.refs_0_, bf16[16,1536]{1,0:T(8,128)(2,1)S(1)} %get-tuple-element.9.refs_1_, bf16[1536,768]{1,0:T(8,128)(2,1)S(1)} %get-tuple-element.10.refs_2_, ...), custom_call_target="tpu_custom_call" | custom-call | tf_op jit(solution)/shard_map/write_out/pallas_call | solution.py:375
